TPU v7x, 512 devices: a whole 4x8x8 slice. The times are simulated.
512 devices in a mesh: replica: 16 (over y, core), shard: 32 (over z, x).
Axes of the slice: x: 4, y: 8, z: 8, core: 2. Of those that a mesh axis runs over, the one named last changes fastest.
Arguments:
- item_table: float32 [65536, 128], P('shard')
- neighbours: int32 [16384, 128], P(('replica', 'shard')), may hold values from 0 to 65535, as said below
- confidence: float32 [16384, 128], P(('replica', 'shard')), may hold values from 0.1 to 10
- valid_counts: int32 [16384], P(('replica', 'shard')), may hold values from 1 to 128, as said below
- row_targets: int32 [16384], P('shard'), may hold values from 0 to 511, as said below
Outputs:
- user_factors: float32 [16384, 128], P('shard')
Inputs may be any that keep to these rules, and one draw needn't show every extreme that they name: `neighbours`: in each aligned block of 32 rows, at most 192 entries lie in any one aligned range of 2048 ids, and this most is reached in every block. `valid_counts`: some row reaches the most. `row_targets`: each aligned block of 512 entries holds every number of its range once.
All inputs are finite; a program needn't handle non-finite values.
Results may differ from a plain program's by a relative error of at most 0.0007.
Values sent between devices are 32-bit elements; how exact they have to be, the bound alone decides.
A program may use at most 64 MiB of HBM per device.

v0:
```python
import jax
import jax.numpy as jnp
from jax import lax
from jax.sharding import PartitionSpec as P

ITERS = 4


HI = lax.Precision.HIGHEST


def conjugate(rhs, scaled, extra_term):
    sol = jnp.zeros_like(rhs)
    resid = rhs
    direc = rhs
    rr_now = jnp.sum(resid * resid, axis=1, keepdims=True)
    for step in range(ITERS):
        image = 1.0 * direc + jnp.dot(direc, scaled, precision=HI) + extra_term(direc)
        alpha = rr_now / jnp.sum(direc * image, axis=1, keepdims=True)
        sol = sol + alpha * direc
        resid = resid - alpha * image
        rr_next = jnp.sum(resid * resid, axis=1, keepdims=True)
        direc = resid + rr_next / rr_now * direc
        rr_now = rr_next
    return sol


def per_device(item_table, neighbours, confidence, valid_counts, row_targets):
    tab_rows, width = item_table.shape
    user_rows, slot_count = neighbours.shape
    nshard = lax.axis_size("shard")
    total_items = tab_rows * nshard
    partial_gram = jnp.dot(item_table.T, item_table, precision=HI)
    gram = lax.psum(partial_gram, "shard")
    scaled = 2.0 / total_items * gram
    used = jnp.arange(slot_count)[None, :] < valid_counts[:, None]
    wmask = jnp.where(used, confidence, 0.0)
    bmask = jnp.where(used, 1.0 + confidence, 0.0)
    root_width = jnp.sqrt(jnp.float32(width))
    flat_ids = neighbours.reshape(-1)
    slots = flat_ids.shape[0]
    cap = slots // nshard + slots // (2 * nshard)
    owner = flat_ids // tab_rows
    local = flat_ids % tab_rows
    onehot_owner = (owner[:, None] == jnp.arange(nshard)[None, :]).astype(jnp.int32)
    before = jnp.cumsum(onehot_owner, axis=0) - onehot_owner
    position = jnp.sum(before * onehot_owner, axis=1)
    slot_index = owner * cap + position
    send_ids = jnp.zeros((nshard * cap,), jnp.int32).at[slot_index].set(local).reshape(nshard, cap)
    found = jnp.take(
        item_table,
        lax.all_to_all(send_ids, "shard", split_axis=0, concat_axis=0, tiled=True),
        axis=0,
    )
    answered = lax.all_to_all(found, "shard", split_axis=0, concat_axis=0, tiled=True)
    fetched = jnp.take(answered.reshape(nshard * cap, width), slot_index, axis=0)
    rows = fetched.reshape(user_rows, slot_count, width)
    rhs = jnp.einsum("uk,ukd->ud", bmask, rows, precision=HI) / root_width

    def slot_term(vec):
        proj = jnp.einsum("ukd,ud->uk", rows, vec, precision=HI)
        coef = wmask * proj / width
        return jnp.einsum("uk,ukd->ud", coef, rows, precision=HI)

    solved = conjugate(rhs, scaled, slot_term)
    gathered = lax.all_gather(solved, "replica", axis=0, tiled=True)
    placed = jnp.zeros((row_targets.shape[0], width), jnp.float32).at[row_targets].set(gathered)
    return placed


def solution(mesh):
    return jax.shard_map(
        per_device,
        mesh=mesh,
        in_specs=(
            P("shard", None),
            P(("replica", "shard"), None),
            P(("replica", "shard"), None),
            P(("replica", "shard")),
            P("shard"),
        ),
        out_specs=P("shard", None),
        check_vma=False,
    )
```

profile of v0, /device:TPU:1, one launch (start us, length us, event | category | flops | bytes accessed | tf_op | source)
XLA Modules:
  0.0 301.4 jit_solution(17315840918248263334)
XLA Ops:
  6.5 0.0 copy-start
  6.5 0.0 copy-start.3
  6.5 0.8 add_select_fusion.2
  7.4 0.7 add_select_fusion
  8.1 0.1 fusion.45
  8.2 9.2 %reduce-window.6 = s32[32,32,128]{2,1,0:T(8,128)S(1)} reduce-window(s32[32,32,128]{2,1,0:T(8,128)S(1)} %fusion.45, s32[]{:T(128)} %constant.69.clone.1), window={size=1x1x128 pad=0_0x0_0x127_0}, to_apply=%region_0.0 | reduce-window | flops 16646144 | bytes 1048580 | tf_op jit(solution)/shard_map/reduce-window
  17.4 0.8 slice_reduce_fusion
  18.2 0.2 reduce-window.9
  18.4 0.2 broadcast_add_fusion
  18.6 0.4 fusion.44
  19.0 0.0 copy-done.3
  19.0 0.1 compare_select_fusion.1
  19.1 15.5 %scatter_custom_fusion = s32[6144]{0:T(1024)S(1)} fusion(s32[4096]{0:T(1024)S(1)} %bitcast.158, s32[4096]{0:T(1024)S(1)} %get-tuple-element.11, s32[]{:T(128)} %constant.69.clone.1), kind=kCustom, calls=%fused_computation.120 | custom fusion | bytes 24580 | tf_op jit(solution)/shard_map/scatter | solution.py:49
  34.6 0.1 all_to_all.13
  34.7 22.2 %all_to_all.20 = s32[32,1,192]{2,1,0:T(1,128)S(1)} all-to-all(s32[32,1,192]{2,1,0:T(1,128)S(1)} %all_to_all.13), channel_id=1, replica_groups=mesh['replica'=16,'shard'=32] {'shard'}, dimensions={0} | all-to-all | bytes 49152 | tf_op jit(solution)/shard_map/all_to_all | solution.py:52
  57.0 0.1 fusion.52
  57.1 0.1 reshape.223
  57.2 0.0 copy-done
  57.2 20.9 %gather_fusion = f32[6144,128]{1,0:T(8,128)} fusion(f32[2048,128]{1,0:T(8,128)S(1)} %copy-done, s32[6144]{0:T(1024)S(1)} %broadcast_clamp_fusion), kind=kCustom, calls=%fused_computation | custom fusion | bytes 6316032 | tf_op jit(solution)/shard_map/jit(_take)/gather | solution.py:50
  78.1 4.6 %broadcast_select_fusion = f32[32,192,128]{2,1,0:T(8,128)} fusion(f32[32,192,128]{2,1,0:T(8,128)} %bitcast.130, pred[32,192]{1,0:T(8,128)(4,1)S(1)} %compare_and_fusion), kind=kLoop, calls=%fused_computation.4 | loop fusion | flops 786432 | bytes 6297600 | tf_op jit(solution)/shard_map/jit(_take)/select_n | solution.py:50
  82.7 4.8 %all-to-all-start.1 = ((f32[32,192,128]{2,1,0:T(8,128)}), f32[32,192,128]{2,1,0:T(8,128)}, u32[]{:S(2)}, u32[]{:S(2)}) async-start(f32[32,192,128]{2,1,0:T(8,128)} %broadcast_select_fusion), calls=%async_computation.1 | async-start | bytes 6291456 | tf_op jit(solution)/shard_map/all_to_all | solution.py:55
  87.5 0.0 copy-start.5
  87.5 0.0 copy-start.2
  87.5 0.0 copy-start.4
  87.6 0.0 all-reduce.2.cloned.1.call-start
  87.6 2.5 fusion.78
  90.1 0.0 all-reduce.2.cloned.1.call-update
  90.1 0.0 copy-done.5
  90.1 0.0 copy-done.2
  90.1 0.0 copy-done.4
  90.1 0.1 add_select_fusion.3
  90.2 67.9 %all-to-all-done.1 = f32[32,192,128]{2,1,0:T(8,128)} async-done(((f32[32,192,128]{2,1,0:T(8,128)}), f32[32,192,128]{2,1,0:T(8,128)}, u32[]{:S(2)}, u32[]{:S(2)}) %all-to-all-start.1) | async-done | bytes 3145760 | tf_op jit(solution)/shard_map/all_to_all | solution.py:55
  158.2 12.7 %gather_fusion.1 = f32[4096,128]{1,0:T(8,128)S(1)} fusion(f32[6144,128]{1,0:T(8,128)} %bitcast.10, s32[4096]{0:T(1024)S(1)} %broadcast_clamp_fusion.1), kind=kCustom, calls=%fused_computation.1 | custom fusion | bytes 4210688 | tf_op jit(solution)/shard_map/jit(_take)/gather | solution.py:56
  170.8 2.3 fusion.22
  173.2 3.6 %fusion.20 = f32[32,1,128]{2,1,0:T(1,128)S(1)} fusion(f32[32,128,1]{1,2,0:T(1,128)S(1)} %bitcast.156, f32[32,128,128]{2,1,0:T(8,128)S(1)} %bitcast.122, pred[32,128]{1,0:T(8,128)(4,1)S(1)} %compare_and_fusion.1), kind=kOutput, calls=%fused_computation.29 | convolution fusion | flops 6815744 | bytes 2134016 | tf_op jit(solution)/shard_map/ukd,ud->uk/dot_general | solution.py:61
  176.8 0.1 multiply_multiply_fusion.3
  176.9 2.3 fusion.18
  179.2 69.7 %all-reduce.2.cloned.1.call-done = f32[128,128]{1,0:T(8,128)} async-done(((f32[128,128]{1,0:T(8,128)}), f32[128,128]{1,0:T(8,128)}) %all-reduce.2.cloned.1.call-update) | async-done | bytes 65552 | tf_op jit(solution)/shard_map/psum | solution.py:34
  248.9 1.1 multiply_reduce_fusion.5
  250.0 0.2 multiply_reduce_fusion.4
  250.2 0.1 multiply_add_fusion.3
  250.3 0.0 copy-start.1
  250.3 3.6 %fusion.16 = f32[32,1,128]{2,1,0:T(1,128)S(1)} fusion(f32[32,128,1]{1,2,0:T(1,128)S(1)} %bitcast.138, f32[32,128,128]{2,1,0:T(8,128)S(1)} %bitcast.124, pred[32,128]{1,0:T(8,128)(4,1)S(1)} %compare_and_fusion.1), kind=kOutput, calls=%fused_computation.25 | convolution fusion | flops 6815744 | bytes 2134016 | tf_op jit(solution)/shard_map/ukd,ud->uk/dot_general | solution.py:61
  254.0 0.1 multiply_multiply_fusion.2
  254.0 2.3 fusion.14
  256.3 0.0 copy-done.1
  256.3 0.3 multiply_reduce_fusion.3
  256.6 0.2 multiply_reduce_fusion.2
  256.8 0.1 multiply_add_fusion.2
  256.9 3.6 %fusion.12 = f32[32,1,128]{2,1,0:T(1,128)S(1)} fusion(f32[32,128,1]{1,2,0:T(1,128)S(1)} %bitcast.139, f32[32,128,128]{2,1,0:T(8,128)S(1)} %bitcast.126, pred[32,128]{1,0:T(8,128)(4,1)S(1)} %compare_and_fusion.1), kind=kOutput, calls=%fused_computation.21 | convolution fusion | flops 6815744 | bytes 2134016 | tf_op jit(solution)/shard_map/ukd,ud->uk/dot_general | solution.py:61
  260.6 0.1 multiply_multiply_fusion.1
  260.6 2.3 fusion.10
  262.9 0.3 multiply_reduce_fusion.1
  263.2 0.2 multiply_reduce_fusion
  263.4 0.1 multiply_add_fusion.1
  263.5 3.6 %fusion.8 = f32[32,1,128]{2,1,0:T(1,128)S(1)} fusion(f32[32,128,1]{1,2,0:T(1,128)S(1)} %bitcast.140, f32[32,128,128]{2,1,0:T(8,128)S(1)} %bitcast.128, pred[32,128]{1,0:T(8,128)(4,1)S(1)} %compare_and_fusion.1), kind=kOutput, calls=%fused_computation.17 | convolution fusion | flops 6815744 | bytes 2134016 | tf_op jit(solution)/shard_map/ukd,ud->uk/dot_general | solution.py:61
  267.2 0.1 multiply_multiply_fusion
  267.2 2.3 fusion.6
  269.6 0.3 fusion.5
  269.8 0.1 multiply_add_fusion
  269.9 22.2 %all_gather.3 = f32[512,128]{1,0:T(8,128)S(1)} all-gather(f32[32,128]{1,0:T(8,128)S(1)} %multiply_add_fusion), channel_id=1, replica_groups=mesh['replica'=16,'shard'=32] {'replica'}, dimensions={0}, use_global_device_ids=true | all-gather | bytes 278528 | tf_op jit(solution)/shard_map/all_gather | solution.py:66
  292.2 2.4 scatter_custom_fusion.1
  (13 shorter events, 0.1 us)
Async XLA Ops:
  6.5 50.6 %copy-start = (f32[2048,128]{1,0:T(8,128)S(1)}, f32[2048,128]{1,0:T(8,128)}, u32[]{:S(2)}) copy-start(f32[2048,128]{1,0:T(8,128)} %param.5) | copy-start | bytes 3145732
  6.5 12.4 %copy-start.3 = (s32[32,128]{1,0:T(8,128)S(1)}, s32[32,128]{1,0:T(8,128)}, u32[]{:S(2)}) copy-start(s32[32,128]{1,0:T(8,128)} %param.6) | copy-start | bytes 49156
  82.7 75.5 %all-to-all-start.1 = ((f32[32,192,128]{2,1,0:T(8,128)}), f32[32,192,128]{2,1,0:T(8,128)}, u32[]{:S(2)}, u32[]{:S(2)}) async-start(f32[32,192,128]{2,1,0:T(8,128)} %broadcast_select_fusion), calls=%async_computation.1 | async-start | bytes 6291456 | tf_op jit(solution)/shard_map/all_to_all | solution.py:55
  87.5 2.6 copy-start.5
  87.5 2.6 copy-start.2
  87.5 2.6 copy-start.4
  87.6 161.3 %all-reduce.2.cloned.1.call-start = ((), (), s32[]{:S(2)}) async-start(), calls=%async_computation.2 | async-start | bytes 131072 | tf_op jit(solution)/shard_map/psum | solution.py:34
  250.3 6.0 %copy-start.1 = (f32[128,128]{1,0:T(8,128)S(1)}, f32[128,128]{1,0:T(8,128)}, u32[]{:S(2)}) copy-start(f32[128,128]{1,0:T(8,128)} %all-reduce.2.cloned.1.call-done) | copy-start | bytes 196612
Sparse Core Ops, SparseCore 0:
  91.8 157.0 all-reduce.1
where the time goes:
time: 302 us; the launch traced here: 301 us
  waiting for transfers between devices  138 us (46%)
  local copies, waits for them, and re-layouts  52.4 us (17%)
  blocking collectives  44.5 us (15%)
  matrix products  30.5 us (10%)
  other arithmetic  17.8 us (6%)
  between operations  13.6 us (5%)
  starting transfers between devices  4.85 us (2%)
    psum x1, waiting for transfers between devices, per_device(): gram = lax.psum(partial_gram, 'shard')  69.7 us
    all_to_all x1, waiting for transfers between devices, per_device(): lax.all_to_all(found, 'shard', split_axis=0, concat_axis=0, tiled=True)  67.9 us
    all_gather x1, blocking collectives, per_device(): gathered = lax.all_gather(solved, 'replica', axis=0, tiled=True)  22.2 us
    all_to_all x1, blocking collectives, per_device(): lax.all_to_all(send_ids, 'shard', split_axis=0, concat_axis=0, tiled=True)  22.2 us
    gather x1, local copies, waits for them, and re-layouts, per_device(): jnp.take(item_table, lax.all_to_all(send_ids, 'shard', split_axis=0, conc...  20.9 us
    scatter x1, local copies, waits for them, and re-layouts, per_device(): jnp.zeros((nshard * cap,), jnp.int32).at[slot_index].set(local)  15.5 us
    dot_general x4, matrix products, slot_term(): proj = jnp.einsum('ukd,ud->uk', rows, vec, precision=HI)  14.6 us
    gather x1, local copies, waits for them, and re-layouts, per_device(): jnp.take(answered.reshape(nshard * cap, width), slot_index, axis=0)  12.7 us
  transfers between devices with their start and end apart: 2, of which 2 were waited for; matrix products, arithmetic and copies ran while one was open for 8% of the time, Pallas kernels for 0%

commit v1 on v0

v1 whole, which is shorter than its diff:
```python
import functools
import math

import jax
import jax.numpy as jnp
from jax import lax
from jax.experimental import pallas as pl
from jax.experimental.pallas import tpu as pltpu
from jax.sharding import PartitionSpec as P

ITERS = 4
NX, NZ, NY = 4, 8, 8
D = 128
K = 128
U = 32
TAB = 2048
ITEMS = 65536
CAP = 192
SLOTS = NX * CAP
KH = SLOTS // 128
MESH = pl.DeviceIdType.MESH
F32, BF16, I32 = jnp.float32, jnp.bfloat16, jnp.int32
ORDER = (1, 7, 2, 6, 3, 5, 4)
NT = (((1,), (1,)), ((), ()))
TN = (((0,), (0,)), ((), ()))


def split2(v):
    hi = v.astype(BF16)
    lo = (v - hi.astype(F32)).astype(BF16)
    return hi, lo


def split3(v):
    hi = v.astype(BF16)
    rest = v - hi.astype(F32)
    mid = rest.astype(BF16)
    lo = (rest - mid.astype(F32)).astype(BF16)
    return hi, mid, lo


def iota(shape, dim):
    return lax.broadcasted_iota(I32, shape, dim)


def kernel(
    counts, ids_ref, conf_ref, targ_ref, table,
    out_ref,
    tab0, tab1, tab2, tab3, code_s, kl_s, val_s, a_s, b_s, ent_send, ent, idv, ids_smem, found, fmat, mw, gacc,
    psend, pbuf, qsend, qbuf, gat, place,
    own_sem, tx_sem, trx_sem, tfwd_sem, ts_sem, tsr_sem, es_sem, er_sem, id_sem, ps_sem, pr_sem, qs_sem, qr_sem,
    ys_sem, yr_sem, ss_sem, sr_sem,
):
    r = lax.axis_index("replica")
    s = lax.axis_index("shard")
    z, x = lax.div(s, NX), lax.rem(s, NX)
    y, core = lax.div(r, 2), lax.rem(r, 2)

    def zpeer(dz):
        return (r, lax.rem(z + dz, NZ) * NX + x)

    def xpeer(dx):
        return (r, z * NX + lax.rem(x + dx, NX))

    def ypeer(dy):
        return (lax.rem(y + dy, NY) * 2 + core, s)

    sibling = (y * 2 + 1 - core, s)

    own = pltpu.make_async_copy(table, tab0, own_sem)
    own.start()

    barrier = pltpu.get_barrier_semaphore()
    peers = [xpeer(1), xpeer(3), sibling]
    peers += [zpeer(dz) for dz in range(1, NZ)] + [ypeer(dy) for dy in range(1, NY)]
    for peer in peers:
        pl.semaphore_signal(barrier, inc=1, device_id=peer, device_id_type=MESH)
    pl.semaphore_wait(barrier, len(peers))

    half = TAB // 2
    piece = half // 2

    def rows_of(c):
        return pl.ds(pl.multiple_of(core * half + c * piece, piece), piece)

    def remote(src, dst, send, recv, peer):
        return pltpu.make_async_remote_copy(
            src_ref=src, dst_ref=dst, send_sem=send, recv_sem=recv, device_id=peer, device_id_type=MESH)

    right = [remote(table.at[rows_of(c)], tab3.at[rows_of(c)], tx_sem.at[c], trx_sem.at[c], xpeer(1)) for c in range(2)]
    left = [remote(table.at[rows_of(c)], tab1.at[rows_of(c)], tx_sem.at[2 + c], trx_sem.at[2 + c], xpeer(3)) for c in range(2)]
    fwd_right = remote(tab3.at[rows_of(0)], tab2.at[rows_of(0)], tfwd_sem.at[0], trx_sem.at[4], xpeer(1))
    fwd_left = remote(tab1.at[rows_of(1)], tab2.at[rows_of(1)], tfwd_sem.at[1], trx_sem.at[5], xpeer(3))
    arrivals = [(tab3, 0), (tab1, 1), (tab3, 1), (tab1, 0), (tab2, 0), (tab2, 1)]
    to_sib = [
        remote(t.at[rows_of(c)], t.at[rows_of(c)], ts_sem.at[i], tsr_sem.at[i], sibling)
        for i, (t, c) in enumerate(arrivals)
    ]
    right[0].start()
    left[1].start()
    right[1].start()
    left[0].start()

    ids = ids_ref[...]
    owner = lax.shift_right_logical(ids, 11)
    local = ids & (TAB - 1)
    rowi = iota((U, K), 0)
    lane = iota((U, K), 1)
    cnt = jnp.zeros((U, K), I32)
    for u in range(U):
        cnt = jnp.where(rowi == u, counts[u], cnt)
    used = lane < cnt
    key = jnp.where(used, owner, -1)
    e_all = jnp.concatenate(
        [jnp.where(key == o, 1.0, 0.0).astype(BF16) for o in range(NX * NZ)], axis=0)
    br, bc = iota((256, 256), 0), iota((256, 256), 1)
    lower = jnp.where((lax.shift_right_logical(br, 5) == lax.shift_right_logical(bc, 5)) & (bc < br), 1.0, 0.0).astype(BF16)
    x_all = jnp.concatenate(
        [jnp.dot(lower, e_all[i * 256:(i + 1) * 256], preferred_element_type=F32).astype(BF16) for i in range(4)], axis=0)
    tr, tc = iota((256, 128), 0), iota((256, 128), 1)
    tri = jnp.where((tr >= 128) | (tr < tc), 1.0, 0.0).astype(BF16)
    pos_all = jnp.dot(jnp.concatenate([e_all, x_all], axis=1), tri, preferred_element_type=F32)
    pos = jnp.zeros((U, K), F32)
    for o in range(NX * NZ):
        pos = jnp.where(key == o, pos_all[o * U:(o + 1) * U], pos)
    slot = (owner & (NX - 1)) * CAP + pos.astype(I32)
    code_s[...] = jnp.where(used, lax.shift_right_logical(owner, 2) * 8 + lax.shift_right_logical(slot, 7), -1)
    kl_s[...] = slot & 127
    conf = conf_ref[...]
    m1, m2, m3 = split3(conf)
    val_s[0] = (local & 0x700).astype(F32)
    val_s[1] = (local & 0xFF).astype(F32)
    val_s[2] = (rowi + 1).astype(F32)
    val_s[3] = m1.astype(F32)
    val_s[4] = m2.astype(F32)
    val_s[5] = m3.astype(F32)
    sub = iota((128, 128), 0)

    def build(u, carry):
        cols = pl.ds(pl.multiple_of(u * 128, 128), 128)
        a_s[:, cols] = jnp.where(sub == code_s[pl.ds(u, 1), :], 1.0, 0.0).astype(BF16)
        hot = sub == kl_s[pl.ds(u, 1), :]
        for c in range(6):
            b_s[c * 128:(c + 1) * 128, cols] = jnp.where(hot, val_s[c, pl.ds(u, 1), :], 0.0).astype(BF16)
        return carry

    lax.fori_loop(0, U, build, 0)
    packed = lax.dot_general(b_s[...], a_s[...], NT, preferred_element_type=F32)
    e_id = (packed[0:128] + packed[128:256]).T[0:64]
    e_user = packed[256:384].T[0:64]
    e_conf = (packed[384:512] + packed[512:640] + packed[640:768]).T[0:64]
    ent_send[:, 0:8, :] = e_id.reshape(NZ, 8, 128)
    ent_send[:, 8:16, :] = e_user.reshape(NZ, 8, 128)
    ent_send[:, 16:24, :] = e_conf.reshape(NZ, 8, 128)
    ent[z] = ent_send[z]
    ent_copies = []
    for i, dz in enumerate(ORDER):
        copy = remote(ent_send.at[lax.rem(z + dz, NZ)], ent.at[z], es_sem.at[i], er_sem.at[i], zpeer(dz))
        copy.start()
        ent_copies.append(copy)

    place[...] = jnp.where(iota((512, 512), 0) == targ_ref[...], 1.0, 0.0).astype(BF16)

    gacc[...] = jnp.zeros_like(gacc)

    def gram_of(tab):
        def step(i, carry):
            v = tab[pl.ds(pl.multiple_of(i * 512, 512), 512), :]
            hl = jnp.concatenate(split2(v), axis=1)
            gacc[...] += lax.dot_general(hl, hl, TN, preferred_element_type=F32)
            return carry
        lax.fori_loop(0, TAB // 512, step, 0)

    own.wait()
    gram_of(tab0)

    right[0].wait_recv()
    fwd_right.start()
    to_sib[0].start()
    left[1].wait_recv()
    fwd_left.start()
    to_sib[1].start()

    for copy in ent_copies:
        copy.wait_recv()
    idv[...] = ent[:, 0:8, :].astype(I32).reshape(NZ * 8, 128) & (TAB - 1)
    idcopy = pltpu.make_async_copy(idv, ids_smem, id_sem)
    idcopy.start()
    ucode = (iota((U, 128), 0) + 1).astype(F32)

    def weights(i, carry):
        for kh in range(KH):
            eq = ent[i, pl.ds(8 + kh, 1), :] == ucode
            m = ent[i, pl.ds(16 + kh, 1), :]
            mw[i, :, kh * 128:(kh + 1) * 128] = jnp.where(eq, m * (1.0 / D), 0.0)
        return carry

    lax.fori_loop(0, NZ, weights, 0)
    idcopy.wait()

    def gather(tab, rel):
        first = lax.rem(x + rel, NX) * CAP

        def step(i, carry):
            src, t = lax.div(i, 3), lax.rem(i, 3)
            k0 = first + t * 64
            row = src * 8 + lax.div(k0, 128)
            col = lax.rem(k0, 128)
            base = src * SLOTS + k0
            for l in range(64):
                found[pl.ds(base + l, 1), :] = tab[pl.ds(ids_smem[row, col + l], 1), :]
            return carry

        lax.fori_loop(0, NZ * 3, step, 0)

    gather(tab0, 0)
    right[1].wait_recv()
    to_sib[2].start()
    left[0].wait_recv()
    to_sib[3].start()
    for i in (0, 2):
        to_sib[i].wait_recv()
    gather(tab3, 3)
    gram_of(tab3)
    for i in (1, 3):
        to_sib[i].wait_recv()
    gather(tab1, 1)
    gram_of(tab1)
    fwd_right.wait_recv()
    to_sib[4].start()
    fwd_left.wait_recv()
    to_sib[5].start()
    for i in (4, 5):
        to_sib[i].wait_recv()
    gather(tab2, 2)
    gram_of(tab2)

    scale = 2.0 / ITEMS
    g = (gacc[0:128, 0:128] + gacc[0:128, 128:256] + gacc[128:256, 0:128] + gacc[128:256, 128:256]) * scale
    ghl = jnp.concatenate(split2(g), axis=1)

    def convert(i, carry):
        for c in range(KH):
            v = found[pl.ds(pl.multiple_of(i * SLOTS + c * 128, 128), 128), :]
            fmat[i, c * 128:(c + 1) * 128, :] = jnp.concatenate(split2(v), axis=1)
        fmat[i, SLOTS:SLOTS + 128, :] = ghl
        return carry

    lax.fori_loop(0, NZ, convert, 0)

    def fold(res):
        return res[0:U, 0:128] + res[0:U, 128:256] + res[U:2 * U, 0:128]

    def rhs_share(i):
        parts = []
        for kh in range(KH):
            eq = ent[i, pl.ds(8 + kh, 1), :] == ucode
            m = ent[i, pl.ds(16 + kh, 1), :]
            parts.append(jnp.where(eq, (1.0 + m) * (1.0 / math.sqrt(D)), 0.0))
        hi, lo = split2(jnp.concatenate(parts, axis=1))
        return fold(jnp.dot(jnp.concatenate([hi, lo], axis=0), fmat[i, 0:SLOTS, :], preferred_element_type=F32))

    def project(i, hi, lo):
        lhs = jnp.concatenate(
            [jnp.concatenate([hi, hi], axis=1), jnp.concatenate([lo, jnp.zeros_like(lo)], axis=1)], axis=0)
        res = lax.dot_general(lhs, fmat[i, 0:SLOTS, :], NT, preferred_element_type=F32)
        return res[0:U] + res[U:2 * U]

    def share(i, p):
        hi, lo = split2(p)
        yhi, ylo = split2(mw[i] * project(i, hi, lo))
        lhs = jnp.concatenate(
            [jnp.concatenate([yhi, hi], axis=1), jnp.concatenate([ylo, lo], axis=1)], axis=0)
        return fold(jnp.dot(lhs, fmat[i], preferred_element_type=F32))

    def last_share(i, p):
        hi, lo = split2(p)
        proj = project(i, hi, lo)
        sq = mw[i] * proj * proj
        t = fold(jnp.dot(jnp.concatenate([hi, lo], axis=0), fmat[i, SLOTS:SLOTS + 128, :], preferred_element_type=F32)) * p
        for kh in range(KH):
            t = t + sq[:, kh * 128:(kh + 1) * 128]
        return t

    p_copies = [remote(psend, pbuf.at[z], ps_sem.at[i], pr_sem.at[i], zpeer(dz)) for i, dz in enumerate(ORDER)]

    def q_copy(i, dz):
        return remote(qsend.at[i], qbuf.at[NZ - dz], qs_sem.at[dz], qr_sem.at[NZ - dz], zpeer(dz))

    q_copies = [q_copy(i, dz) for i, dz in enumerate(ORDER)]

    def exchange(fn, p):
        if p is not None:
            psend[...] = p
            for copy in reversed(p_copies):
                copy.start()
        total = fn(z, p)
        for i, dz in enumerate(ORDER):
            src = lax.rem(z + dz, NZ)
            if p is not None:
                p_copies[ORDER.index(NZ - dz)].wait_recv()
                theirs = pbuf[src]
            else:
                theirs = None
            qsend[i] = fn(src, theirs)
            q_copies[i].start()
        for i in range(len(ORDER)):
            q_copies[i].wait_recv()
        for dz in range(1, NZ):
            total = total + qbuf[dz]
        for copy in q_copies:
            copy.wait_send()
        if p is not None:
            for copy in p_copies:
                copy.wait_send()
        return total

    rhs = exchange(lambda i, p: rhs_share(i), None)

    def norm(v):
        return jnp.sum(v * v, axis=1, keepdims=True)

    def iterate(_, carry):
        sol, res, p, rr = carry
        q = p + exchange(share, p)
        alpha = rr / jnp.sum(p * q, axis=1, keepdims=True)
        sol = sol + alpha * p
        res = res - alpha * q
        new = norm(res)
        return sol, res, res + (new / rr) * p, new

    carry = (jnp.zeros_like(rhs), rhs, rhs, norm(rhs))
    sol, res, p, rr = lax.fori_loop(0, ITERS - 1, iterate, carry)
    pq = jnp.sum(p * p + exchange(last_share, p), axis=1, keepdims=True)
    sol = sol + (rr / pq) * p

    def group_rows(dy, c):
        return pl.ds(pl.multiple_of((lax.rem(y + dy, NY) * 2 + c) * U, U), U)

    gat[group_rows(0, core), :] = sol
    mine = gat.at[group_rows(0, core)]
    y_copies = [remote(mine, mine, ys_sem.at[dy], yr_sem.at[dy], ypeer(dy)) for dy in range(1, NY)]
    s_copies = [
        remote(gat.at[group_rows(dy, core)], gat.at[group_rows(dy, core)], ss_sem.at[dy], sr_sem.at[dy], sibling)
        for dy in range(NY)
    ]
    for copy in reversed(y_copies):
        copy.start()
    s_copies[0].start()
    for dy in (1, 7, 2, 6, 3, 5, 4):
        y_copies[NY - dy - 1].wait_recv()
        s_copies[dy].start()
    for copy in s_copies:
        copy.wait_recv()
    hml = jnp.concatenate(split3(gat[...]), axis=1)
    placed = jnp.dot(place[...], hml, preferred_element_type=F32)
    out_ref[...] = placed[:, 0:128] + placed[:, 128:256] + placed[:, 256:384]

    for copy in right + left + [fwd_right, fwd_left] + to_sib + ent_copies + y_copies + s_copies:
        copy.wait_send()


def per_device(item_table, neighbours, confidence, valid_counts, row_targets):
    vmem = pl.BlockSpec(memory_space=pltpu.VMEM)
    dma = pltpu.SemaphoreType.DMA
    return pl.pallas_call(
        kernel,
        out_shape=jax.ShapeDtypeStruct((512, D), F32),
        in_specs=[pl.BlockSpec(memory_space=pltpu.SMEM), vmem, vmem, vmem, pl.BlockSpec(memory_space=pl.ANY)],
        out_specs=vmem,
        scratch_shapes=[
            pltpu.VMEM((TAB, D), F32), pltpu.VMEM((TAB, D), F32), pltpu.VMEM((TAB, D), F32), pltpu.VMEM((TAB, D), F32),
            pltpu.VMEM((U, K), I32), pltpu.VMEM((U, K), I32), pltpu.VMEM((6, U, K), F32),
            pltpu.VMEM((128, U * K), BF16), pltpu.VMEM((6 * 128, U * K), BF16),
            pltpu.VMEM((NZ, 24, 128), F32), pltpu.VMEM((NZ, 24, 128), F32),
            pltpu.VMEM((NZ * 8, 128), I32), pltpu.SMEM((NZ * 8, 128), I32),
            pltpu.VMEM((NZ * SLOTS, D), F32), pltpu.VMEM((NZ, SLOTS + 128, 2 * D), BF16),
            pltpu.VMEM((NZ, U, SLOTS), F32), pltpu.VMEM((2 * D, 2 * D), F32),
            pltpu.VMEM((U, D), F32), pltpu.VMEM((NZ, U, D), F32),
            pltpu.VMEM((NZ - 1, U, D), F32), pltpu.VMEM((NZ, U, D), F32),
            pltpu.VMEM((512, D), F32), pltpu.VMEM((512, 512), BF16),
            dma, dma((4,)), dma((6,)), dma((2,)), dma((6,)), dma((6,)), dma((7,)), dma((7,)), dma,
            dma((7,)), dma((7,)), dma((NZ,)), dma((NZ,)), dma((NY,)), dma((NY,)), dma((NY,)), dma((NY,)),
        ],
        compiler_params=pltpu.CompilerParams(
            collective_id=0, has_side_effects=True, vmem_limit_bytes=48 * 1024 * 1024),
    )(valid_counts, neighbours, confidence, row_targets.reshape(1, 512), item_table)


def solution(mesh):
    return jax.shard_map(
        per_device,
        mesh=mesh,
        in_specs=(
            P("shard", None),
            P(("replica", "shard"), None),
            P(("replica", "shard"), None),
            P(("replica", "shard")),
            P("shard"),
        ),
        out_specs=P("shard", None),
        check_vma=False,
    )
```

time: 302 us -> 117 us (0.39)
  waiting for transfers between devices: 138 us -> 0 us
  Pallas kernels: 0 us -> 112 us
  local copies, waits for them, and re-layouts: 52.4 us -> 4.7 us
  blocking collectives: 44.5 us -> 0 us
  matrix products: 30.5 us -> 0 us
  other arithmetic: 17.8 us -> 0 us
  between operations: 13.6 us -> 0.01 us
  starting transfers between devices: 4.85 us -> 0 us
    pallas_call x0 -> x1, Pallas kernels: none -> 112 us  [per_device(): pl.pallas_call(kernel, out_shape=jax.ShapeDtypeStruct((512, D), F32), in_...]
    psum x1 -> x0, waiting for transfers between devices: 69.7 us -> none  [per_device(): gram = lax.psum(partial_gram, 'shard')]
    all_to_all x1 -> x0, waiting for transfers between devices: 67.9 us -> none  [per_device(): lax.all_to_all(found, 'shard', split_axis=0, concat_axis=0, tiled=True)]
    gather x2 -> x0, local copies, waits for them, and re-layouts: 33.5 us -> none  [the longest x1 20.9 us: per_device(): jnp.take(item_table, lax.all_to_all(send_ids, 'shard', split_axis=0, conc...]
    dot_general x14 -> x0, matrix products: 30.5 us -> none  [the longest x4 14.6 us: slot_term(): proj = jnp.einsum('ukd,ud->uk', rows, vec, precision=HI)]
    all_gather x1 -> x0, blocking collectives: 22.2 us -> none  [per_device(): gathered = lax.all_gather(solved, 'replica', axis=0, tiled=True)]
    all_to_all x1 -> x0, blocking collectives: 22.2 us -> none  [per_device(): lax.all_to_all(send_ids, 'shard', split_axis=0, concat_axis=0, tiled=True)]
    scatter x2 -> x0, local copies, waits for them, and re-layouts: 17.9 us -> none  [the longest x1 15.5 us: per_device(): jnp.zeros((nshard * cap,), jnp.int32).at[slot_index].set(local)]
  transfers between devices with their start and end apart: 2 -> 0, of which waited for: 2 -> 0; matrix products, arithmetic and copies ran while one was open for 8% -> 0% of each run, Pallas kernels for 0% -> 0%
where the time goes in v1:
time: 117 us
  Pallas kernels  112 us (96%)
  local copies, waits for them, and re-layouts  4.7 us (4%)
    pallas_call x1, Pallas kernels, per_device(): pl.pallas_call(kernel, out_shape=jax.ShapeDtypeStruct((512, D), F32), in_...  112 us
    unnamed x11, local copies, waits for them, and re-layouts  4.7 us

profile of v1, /device:TPU:1, one launch (start us, length us, event | category | flops | bytes accessed | tf_op | source)
XLA Modules:
  0.0 116.7 jit_solution(1293059370285818898)
XLA Ops:
  0.0 0.0 copy-start.4
  0.0 0.7 copy-done.4
  0.7 0.0 copy-start
  0.7 1.2 %copy-done = f32[2048,128]{1,0:T(8,128)S(1)} copy-done((f32[2048,128]{1,0:T(8,128)S(1)}, f32[2048,128]{1,0:T(8,128)}, u32[]{:S(2)}) %copy-start) | copy-done | bytes 1048600
  1.9 0.0 copy-start.1
  1.9 0.7 copy-done.1
  2.6 0.0 copy-start.2
  2.6 0.7 copy-done.2
  3.3 0.0 copy-start.3
  3.3 0.7 copy-done.3
  4.0 111.9 %shard_map.55 = f32[512,128]{1,0:T(8,128)S(1)} custom-call(s32[32]{0:T(128)S(1)} %copy-done.4, s32[32,128]{1,0:T(8,128)S(1)} %copy-done.1, f32[32,128]{1,0:T(8,128)S(1)} %copy-done.2, s32[1,512]{1,0:T(1,128)S(1)} %bitcast.1, f32[2048,128]{1,0:T(8,128)S(1)} %copy-done), custom_call_target="tpu_custom_call" | custom-call | tf_op jit(solution)/shard_map/pallas_call | solution.py:366
  115.9 0.7 copy.7
Async XLA Ops:
  0.0 0.7 copy-start.4
  0.7 1.2 %copy-start = (f32[2048,128]{1,0:T(8,128)S(1)}, f32[2048,128]{1,0:T(8,128)}, u32[]{:S(2)}) copy-start(f32[2048,128]{1,0:T(8,128)} %table.1) | copy-start | bytes 3145732
  1.9 0.7 copy-start.1
  2.6 0.7 copy-start.2
  3.3 0.7 copy-start.3

commit v2 on v1

v2 whole, which is shorter than its diff:
```python
import math

import jax
import jax.numpy as jnp
from jax import lax
from jax.experimental import pallas as pl
from jax.experimental.pallas import tpu as pltpu
from jax.sharding import PartitionSpec as P

ITERS = 4
NX, NZ, NY = 4, 8, 8
D = 128
K = 128
U = 32
TAB = 2048
ITEMS = 65536
CAP = 192
SLOTS = NX * CAP
KH = SLOTS // 128
MESH = pl.DeviceIdType.MESH
F32, BF16, I32 = jnp.float32, jnp.bfloat16, jnp.int32
ORDER = (1, 7, 2, 6, 3, 5, 4)
FAR = (4, 3, 5, 2, 6, 1, 7)
GROUPS = ((1, 7), (2, 6), (3, 5), (4,))
NT = (((1,), (1,)), ((), ()))
TN = (((0,), (0,)), ((), ()))


def split2(v):
    hi = v.astype(BF16)
    lo = (v - hi.astype(F32)).astype(BF16)
    return hi, lo


def split3(v):
    hi = v.astype(BF16)
    rest = v - hi.astype(F32)
    mid = rest.astype(BF16)
    lo = (rest - mid.astype(F32)).astype(BF16)
    return hi, mid, lo


def iota(shape, dim):
    return lax.broadcasted_iota(I32, shape, dim)


def kernel(
    counts_hbm, ids_hbm, conf_hbm, targ_hbm, table,
    out_ref,
    counts, ids_ref, conf_ref, targ_ref,
    tab0, tab1, tab2, tab3, code_s, kl_s, val_s, a_s, b_s, ent_send, ent, ent2, idr, tt, halves, ft, mw, mb, gacc,
    psend, pbuf, qsend, qbuf, gat, place,
    in_sem, own_sem, tx_sem, trx_sem, tfwd_sem, ts_sem, tsr_sem, es_sem, er_sem, ps_sem, pr_sem, qs_sem, qr_sem,
    ys_sem, yr_sem, ss_sem, sr_sem,
):
    r = lax.axis_index("replica")
    s = lax.axis_index("shard")
    z, x = lax.div(s, NX), lax.rem(s, NX)
    y, core = lax.div(r, 2), lax.rem(r, 2)

    def zpeer(dz):
        return (r, lax.rem(z + dz, NZ) * NX + x)

    def xpeer(dx):
        return (r, z * NX + lax.rem(x + dx, NX))

    def ypeer(dy):
        return (lax.rem(y + dy, NY) * 2 + core, s)

    sibling = (y * 2 + 1 - core, s)

    barrier = pltpu.get_barrier_semaphore()
    peers = [zpeer(dz) for dz in range(1, NZ)] + [xpeer(1), xpeer(3), sibling]
    peers += [ypeer(dy) for dy in range(1, NY)]
    for peer in peers:
        pl.semaphore_signal(barrier, inc=1, device_id=peer, device_id_type=MESH)

    loads = [
        pltpu.make_async_copy(src, dst, in_sem.at[i])
        for i, (src, dst) in enumerate(
            [(ids_hbm, ids_ref), (counts_hbm, counts), (conf_hbm, conf_ref), (targ_hbm, targ_ref)])
    ]
    own = pltpu.make_async_copy(table, tab0, own_sem)
    for load in loads:
        load.start()
    own.start()

    half = TAB // 2
    piece = half // 2

    def rows_of(c):
        return pl.ds(pl.multiple_of(core * half + c * piece, piece), piece)

    def remote(src, dst, send, recv, peer):
        return pltpu.make_async_remote_copy(
            src_ref=src, dst_ref=dst, send_sem=send, recv_sem=recv, device_id=peer, device_id_type=MESH)

    right = [remote(table.at[rows_of(c)], tab3.at[rows_of(c)], tx_sem.at[c], trx_sem.at[c], xpeer(1)) for c in range(2)]
    left = [remote(table.at[rows_of(c)], tab1.at[rows_of(c)], tx_sem.at[2 + c], trx_sem.at[2 + c], xpeer(3)) for c in range(2)]
    fwd_right = remote(tab3.at[rows_of(0)], tab2.at[rows_of(0)], tfwd_sem.at[0], trx_sem.at[4], xpeer(1))
    fwd_left = remote(tab1.at[rows_of(1)], tab2.at[rows_of(1)], tfwd_sem.at[1], trx_sem.at[5], xpeer(3))
    arrivals = [(tab3, 0), (tab1, 1), (tab3, 1), (tab1, 0), (tab2, 0), (tab2, 1)]
    to_sib = [
        remote(t.at[rows_of(c)], t.at[rows_of(c)], ts_sem.at[i], tsr_sem.at[i], sibling)
        for i, (t, c) in enumerate(arrivals)
    ]

    for load in loads[:3]:
        load.wait()
    ids = ids_ref[...]
    owner = lax.shift_right_logical(ids, 11)
    local = ids & (TAB - 1)
    rowi = iota((U, K), 0)
    lane = iota((U, K), 1)
    cnt = jnp.zeros((U, K), I32)
    for u in range(U):
        cnt = jnp.where(rowi == u, counts[u], cnt)
    used = lane < cnt
    key = jnp.where(used, owner, -1)
    e_all = jnp.concatenate(
        [jnp.where(key == o, 1.0, 0.0).astype(BF16) for o in range(NX * NZ)], axis=0)
    br, bc = iota((256, 256), 0), iota((256, 256), 1)
    lower = jnp.where((lax.shift_right_logical(br, 5) == lax.shift_right_logical(bc, 5)) & (bc < br), 1.0, 0.0).astype(BF16)
    x_all = jnp.concatenate(
        [jnp.dot(lower, e_all[i * 256:(i + 1) * 256], preferred_element_type=F32).astype(BF16) for i in range(4)], axis=0)
    tr, tc = iota((256, 128), 0), iota((256, 128), 1)
    tri = jnp.where((tr >= 128) | (tr < tc), 1.0, 0.0).astype(BF16)
    pos_all = jnp.dot(jnp.concatenate([e_all, x_all], axis=1), tri, preferred_element_type=F32)
    pos = jnp.zeros((U, K), F32)
    for o in range(NX * NZ):
        pos = jnp.where(key == o, pos_all[o * U:(o + 1) * U], pos)
    pos = pos.astype(I32)
    ox = owner & (NX - 1)
    full = pos < 128
    part = jnp.where(full, lax.shift_right_logical(pos, 6), ox & 1)
    row = jnp.where(full, ox, NX + lax.shift_right_logical(ox, 1))
    code_s[...] = jnp.where(used, part * 64 + lax.shift_right_logical(owner, 2) * 8 + row, -1)
    kl_s[...] = pos & 63
    m1, m2, m3 = split3(conf_ref[...])
    val_s[0] = (local & 0x700).astype(F32)
    val_s[1] = (local & 0xFF).astype(F32)
    val_s[2] = (rowi + 1).astype(F32)
    val_s[3] = m1.astype(F32)
    val_s[4] = m2.astype(F32)
    val_s[5] = m3.astype(F32)
    sub = iota((128, 128), 0)

    def build(u, carry):
        cols = pl.ds(pl.multiple_of(u * 128, 128), 128)
        a_s[:, cols] = jnp.where(sub == code_s[pl.ds(u, 1), :], 1.0, 0.0).astype(BF16)
        hot = sub[0:64] == kl_s[pl.ds(u, 1), :]
        for c in range(6):
            b_s[c * 64:(c + 1) * 64, cols] = jnp.where(hot, val_s[c, pl.ds(u, 1), :], 0.0).astype(BF16)
        return carry

    lax.fori_loop(0, U, build, 0)
    packed = lax.dot_general(b_s[...], a_s[...], NT, preferred_element_type=F32)

    def tiles(v):
        return jnp.concatenate([v[:, 0:64], v[:, 64:128]], axis=0).T.reshape(NZ, 8, 128)

    ent_send[:, 0:8, :] = tiles(packed[0:64] + packed[64:128])
    ent_send[:, 8:16, :] = tiles(packed[128:192])
    ent_send[:, 16:24, :] = tiles(packed[192:256] + packed[256:320] + packed[320:384])
    ent[z] = ent_send[z]

    pl.semaphore_wait(barrier, len(peers))
    ent_copies = [
        remote(ent_send.at[lax.rem(z + dz, NZ)], ent.at[z], es_sem.at[i], er_sem.at[i], zpeer(dz))
        for i, dz in enumerate(ORDER)
    ]
    for copy in reversed(ent_copies):
        copy.start()
    right[0].start()
    left[1].start()
    right[1].start()
    left[0].start()

    loads[3].wait()
    place[...] = jnp.where(iota((512, 512), 0) == targ_ref[...], 1.0, 0.0).astype(BF16)

    def transpose(tab, first):
        for c in range(TAB // 128):
            hi, lo = split2(tab[c * 128:(c + 1) * 128, :].T)
            tt[0:128, c * 128:(c + 1) * 128] = hi
            tt[128:256, c * 128:(c + 1) * 128] = lo
        g = lax.dot_general(tt[...], tt[...], NT, preferred_element_type=F32)
        if first:
            gacc[...] = g
        else:
            gacc[...] += g

    own.wait()
    transpose(tab0, True)

    for copy in ent_copies:
        copy.wait_recv()

    xr = [lax.rem(x + rel, NX) for rel in range(NX)]
    for i in range(NZ):
        ent2[0, i] = ent[i]
        ent2[1, i] = pltpu.roll(ent[i], 64, 1)
    low = iota((1, 128), 1) < 64

    def full_row(i, c, rel):
        return ent[i, pl.ds(c * 8 + xr[rel], 1), :]

    def half_row(i, c, rel, d):
        return ent2[lax.rem(xr[rel] + d, 2), i, pl.ds(c * 8 + NX + lax.div(xr[rel], 2), 1), :]

    for rel in range(NX):
        for g in range(2):
            row = rel * 2 + g
            for t in range(4):
                idr[row:row + 1, t * 128:(t + 1) * 128] = full_row(4 * g + t, 0, rel)
            for t in range(2):
                a = 4 * g + 2 * t
                first, second = (a, a + 1) if rel % 2 == 0 else (a + 1, a)
                idr[row:row + 1, 512 + t * 128:640 + t * 128] = jnp.where(
                    low, half_row(first, 0, rel, 0), half_row(second, 0, rel, 1))

    ucode = (iota((U, 128), 0) + 1).astype(F32)
    for i in range(NZ):
        for t in range(KH):
            if t < NX:
                user, m = full_row(i, 1, t), full_row(i, 2, t)
            else:
                pair = 2 * (t - NX)
                first, second = (pair, pair + 1) if i % 2 == 0 else (pair + 1, pair)
                user = jnp.where(low, half_row(i, 1, first, 0), half_row(i, 1, second, 1))
                m = jnp.where(low, half_row(i, 2, first, 0), half_row(i, 2, second, 1))
            eq = user == ucode
            mw[i, :, t * 128:(t + 1) * 128] = jnp.where(eq, m * (1.0 / D), 0.0)
            mb[i, :, t * 128:(t + 1) * 128] = jnp.where(eq, (1.0 + m) * (1.0 / math.sqrt(D)), 0.0)

    def collect(rel, other):
        def group(g, carry):
            wanted = idr[pl.ds(rel * 2 + g, 1), :]
            item = iota((256, SLOTS), 0).astype(F32)
            acc = None
            for b in range(TAB // 256):
                hot = jnp.where(item == wanted - b * 256.0, 1.0, 0.0).astype(BF16)
                d = jnp.dot(tt[:, b * 256:(b + 1) * 256], hot, preferred_element_type=F32)
                acc = d if acc is None else acc + d
            for t in range(4):
                ft[4 * g + t, :, rel * 128:(rel + 1) * 128] = acc[:, t * 128:(t + 1) * 128].astype(BF16)
            for t in range(2):
                now = acc[:, 512 + t * 128:640 + t * 128]
                if other is None:
                    halves[2 * g + t] = now
                else:
                    then = halves[2 * g + t]
                    even, odd = (now, then) if rel % 2 == 0 else (then, now)
                    keep = iota((256, 128), 1) < 64
                    cols = slice((NX + rel // 2) * 128, (NX + rel // 2 + 1) * 128)
                    ft[4 * g + 2 * t, :, cols] = jnp.where(keep, even, odd).astype(BF16)
                    ft[4 * g + 2 * t + 1, :, cols] = jnp.where(keep, odd, even).astype(BF16)
            return carry

        lax.fori_loop(0, 2, group, 0)

    right[0].wait_recv()
    fwd_right.start()
    to_sib[0].start()
    left[1].wait_recv()
    fwd_left.start()
    to_sib[1].start()
    collect(0, None)
    left[0].wait_recv()
    to_sib[3].start()
    right[1].wait_recv()
    to_sib[2].start()
    for i in (1, 3):
        to_sib[i].wait_recv()
    transpose(tab1, False)
    collect(1, 0)
    for i in (0, 2):
        to_sib[i].wait_recv()
    transpose(tab3, False)
    fwd_right.wait_recv()
    to_sib[4].start()
    fwd_left.wait_recv()
    to_sib[5].start()
    collect(3, None)
    for i in (4, 5):
        to_sib[i].wait_recv()
    transpose(tab2, False)
    collect(2, 3)

    scale = 2.0 / ITEMS
    g = (gacc[0:128, 0:128] + gacc[0:128, 128:256] + gacc[128:256, 0:128] + gacc[128:256, 128:256]) * scale
    ghl = jnp.concatenate(split2(g), axis=0)
    for i in range(NZ):
        ft[i, :, SLOTS:SLOTS + 128] = ghl

    def fold(res):
        return res[0:U, 0:128] + res[0:U, 128:256] + res[U:2 * U, 0:128]

    def rhs_share(i):
        hi, lo = split2(mb[i])
        return fold(lax.dot_general(
            jnp.concatenate([hi, lo], axis=0), ft[i, :, 0:SLOTS], NT, preferred_element_type=F32))

    def project(i, hi, lo):
        lhs = jnp.concatenate(
            [jnp.concatenate([hi, hi], axis=1), jnp.concatenate([lo, jnp.zeros_like(lo)], axis=1)], axis=0)
        res = jnp.dot(lhs, ft[i, :, 0:SLOTS], preferred_element_type=F32)
        return res[0:U] + res[U:2 * U]

    def share(i, p):
        hi, lo = split2(p)
        yhi, ylo = split2(mw[i] * project(i, hi, lo))
        lhs = jnp.concatenate(
            [jnp.concatenate([yhi, hi], axis=1), jnp.concatenate([ylo, lo], axis=1)], axis=0)
        return fold(lax.dot_general(lhs, ft[i], NT, preferred_element_type=F32))

    def last_share(i, p):
        hi, lo = split2(p)
        proj = project(i, hi, lo)
        sq = mw[i] * proj * proj
        t = fold(lax.dot_general(
            jnp.concatenate([hi, lo], axis=0), ft[i, :, SLOTS:SLOTS + 128], NT, preferred_element_type=F32)) * p
        for kh in range(KH):
            t = t + sq[:, kh * 128:(kh + 1) * 128]
        block = lax.shift_right_logical(iota((8, 128), 1), 5)
        folded = jnp.zeros((8, 128), F32)
        for c in range(4):
            v = t[c * 8:(c + 1) * 8]
            v = v + pltpu.roll(v, 64, 1)
            v = v + pltpu.roll(v, 32, 1)
            folded = jnp.where(block == c, v, folded)
        return folded

    p_copies = {dz: remote(psend, pbuf.at[z], ps_sem.at[dz], pr_sem.at[dz], zpeer(dz)) for dz in ORDER}
    q_copies = {
        dz: remote(qsend.at[dz], qbuf.at[NZ - dz], qs_sem.at[dz], qr_sem.at[NZ - dz], zpeer(dz)) for dz in ORDER}
    t_copies = {
        dz: remote(qsend.at[dz, 0:8], qbuf.at[NZ - dz, 0:8], qs_sem.at[dz], qr_sem.at[NZ - dz], zpeer(dz))
        for dz in ORDER}

    def answer(group, fn, copies, rows):
        shares = [fn(lax.rem(z + dz, NZ), dz) for dz in group]
        for dz, value in zip(group, shares):
            qsend[dz, 0:rows] = value
            copies[dz].start()

    def collect_shares(total, copies, rows):
        for dz in ORDER:
            copies[dz].wait_recv()
        for dz in range(1, NZ):
            total = total + qbuf[dz, 0:rows]
        for dz in ORDER:
            copies[dz].wait_send()
        return total

    def exchange(fn, p, copies, rows):
        psend[...] = p
        for dz in FAR:
            p_copies[dz].start()
        total = fn(z, p)
        for group in GROUPS:
            for dz in group:
                p_copies[NZ - dz].wait_recv()
            answer(group, lambda i, dz: fn(i, pbuf[i]), copies, rows)
        total = collect_shares(total, copies, rows)
        for dz in ORDER:
            p_copies[dz].wait_send()
        return total

    answer((4, 3, 5), lambda i, dz: rhs_share(i), q_copies, U)
    answer((2, 6, 1, 7), lambda i, dz: rhs_share(i), q_copies, U)
    rhs = collect_shares(rhs_share(z), q_copies, U)

    def norm(v):
        return jnp.sum(v * v, axis=1, keepdims=True)

    def iterate(_, carry):
        sol, res, p, rr = carry
        q = p + exchange(share, p, q_copies, U)
        alpha = rr / jnp.sum(p * q, axis=1, keepdims=True)
        sol = sol + alpha * p
        res = res - alpha * q
        new = norm(res)
        return sol, res, res + (new / rr) * p, new

    carry = (jnp.zeros_like(rhs), rhs, rhs, norm(rhs))
    sol, res, p, rr = lax.fori_loop(0, ITERS - 1, iterate, carry)
    folded = exchange(last_share, p, t_copies, 8)
    block = lax.shift_right_logical(iota((8, 128), 1), 5)
    pq = norm(p) + jnp.concatenate(
        [jnp.sum(jnp.where(block == c, folded, 0.0), axis=1, keepdims=True) for c in range(4)], axis=0)
    sol = sol + (rr / pq) * p

    def group_rows(dy, c):
        return pl.ds(pl.multiple_of((lax.rem(y + dy, NY) * 2 + c) * U, U), U)

    gat[group_rows(0, core), :] = sol
    mine = gat.at[group_rows(0, core)]
    y_copies = [remote(mine, mine, ys_sem.at[dy], yr_sem.at[dy], ypeer(dy)) for dy in range(1, NY)]
    s_copies = [
        remote(gat.at[group_rows(dy, core)], gat.at[group_rows(dy, core)], ss_sem.at[dy], sr_sem.at[dy], sibling)
        for dy in range(NY)
    ]
    for copy in reversed(y_copies):
        copy.start()
    s_copies[0].start()
    for dy in (1, 7, 2, 6, 3, 5, 4):
        y_copies[NY - dy - 1].wait_recv()
        s_copies[dy].start()
    for copy in s_copies:
        copy.wait_recv()
    hml = jnp.concatenate(split3(gat[...]), axis=1)
    placed = jnp.dot(place[...], hml, preferred_element_type=F32)
    out_ref[...] = placed[:, 0:128] + placed[:, 128:256] + placed[:, 256:384]

    for copy in right + left + [fwd_right, fwd_left] + to_sib + ent_copies + y_copies + s_copies:
        copy.wait_send()


def per_device(item_table, neighbours, confidence, valid_counts, row_targets):
    dma = pltpu.SemaphoreType.DMA
    return pl.pallas_call(
        kernel,
        out_shape=jax.ShapeDtypeStruct((512, D), F32),
        in_specs=[pl.BlockSpec(memory_space=pltpu.HBM)] * 5,
        out_specs=pl.BlockSpec(memory_space=pltpu.VMEM),
        scratch_shapes=[
            pltpu.SMEM((U,), I32), pltpu.VMEM((U, K), I32), pltpu.VMEM((U, K), F32), pltpu.VMEM((1, 512), I32),
            pltpu.VMEM((TAB, D), F32), pltpu.VMEM((TAB, D), F32), pltpu.VMEM((TAB, D), F32), pltpu.VMEM((TAB, D), F32),
            pltpu.VMEM((U, K), I32), pltpu.VMEM((U, K), I32), pltpu.VMEM((6, U, K), F32),
            pltpu.VMEM((128, U * K), BF16), pltpu.VMEM((6 * 64, U * K), BF16),
            pltpu.VMEM((NZ, 24, 128), F32), pltpu.VMEM((NZ, 24, 128), F32), pltpu.VMEM((2, NZ, 24, 128), F32),
            pltpu.VMEM((2 * NX, SLOTS), F32), pltpu.VMEM((2 * D, TAB), BF16), pltpu.VMEM((4, 2 * D, 128), F32),
            pltpu.VMEM((NZ, 2 * D, SLOTS + 128), BF16),
            pltpu.VMEM((NZ, U, SLOTS), F32), pltpu.VMEM((NZ, U, SLOTS), F32), pltpu.VMEM((2 * D, 2 * D), F32),
            pltpu.VMEM((U, D), F32), pltpu.VMEM((NZ, U, D), F32),
            pltpu.VMEM((NZ, U, D), F32), pltpu.VMEM((NZ, U, D), F32),
            pltpu.VMEM((512, D), F32), pltpu.VMEM((512, 512), BF16),
            dma((4,)), dma, dma((4,)), dma((6,)), dma((2,)), dma((6,)), dma((6,)), dma((7,)), dma((7,)),
            dma((NZ,)), dma((NZ,)), dma((NZ,)), dma((NZ,)), dma((NY,)), dma((NY,)), dma((NY,)), dma((NY,)),
        ],
        compiler_params=pltpu.CompilerParams(
            collective_id=0, has_side_effects=True, vmem_limit_bytes=48 * 1024 * 1024),
    )(valid_counts, neighbours, confidence, row_targets.reshape(1, 512), item_table)


def solution(mesh):
    return jax.shard_map(
        per_device,
        mesh=mesh,
        in_specs=(
            P("shard", None),
            P(("replica", "shard"), None),
            P(("replica", "shard"), None),
            P(("replica", "shard")),
            P("shard"),
        ),
        out_specs=P("shard", None),
        check_vma=False,
    )
```

time: 117 us -> 107 us (0.915)
  Pallas kernels: 112 us -> 102 us
    pallas_call x1, Pallas kernels: 112 us -> 102 us  [per_device(): pl.pallas_call(kernel, out_shape=jax.ShapeDtypeStruct((512, D), F32), in_...]
where the time goes in v2:
time: 107 us
  Pallas kernels  102 us (95%)
  local copies, waits for them, and re-layouts  4.7 us (4%)
    pallas_call x1, Pallas kernels, per_device(): pl.pallas_call(kernel, out_shape=jax.ShapeDtypeStruct((512, D), F32), in_...  102 us
    unnamed x11, local copies, waits for them, and re-layouts  4.7 us

profile of v2, /device:TPU:1, one launch (start us, length us, event | category | flops | bytes accessed | tf_op | source)
XLA Modules:
  0.0 106.9 jit_solution(18183906792606611447)
XLA Ops:
  0.0 0.0 copy-start.4
  0.0 0.7 copy-done.4
  0.7 0.0 copy-start
  0.7 1.2 %copy-done = f32[2048,128]{1,0:T(8,128)S(1)} copy-done((f32[2048,128]{1,0:T(8,128)S(1)}, f32[2048,128]{1,0:T(8,128)}, u32[]{:S(2)}) %copy-start) | copy-done | bytes 1048600
  1.9 0.0 copy-start.1
  1.9 0.7 copy-done.1
  2.6 0.0 copy-start.2
  2.6 0.7 copy-done.2
  3.3 0.0 copy-start.3
  3.3 0.7 copy-done.3
  4.0 102.2 %shard_map.55 = f32[512,128]{1,0:T(8,128)S(1)} custom-call(s32[32]{0:T(128)S(1)} %copy-done.4, s32[32,128]{1,0:T(8,128)S(1)} %copy-done.1, f32[32,128]{1,0:T(8,128)S(1)} %copy-done.2, s32[1,512]{1,0:T(1,128)S(1)} %bitcast.1, f32[2048,128]{1,0:T(8,128)S(1)} %copy-done), custom_call_target="tpu_custom_call" | custom-call | tf_op jit(solution)/shard_map/pallas_call | solution.py:422
  106.2 0.7 copy.7
Async XLA Ops:
  0.0 0.7 copy-start.4
  0.7 1.2 %copy-start = (f32[2048,128]{1,0:T(8,128)S(1)}, f32[2048,128]{1,0:T(8,128)}, u32[]{:S(2)}) copy-start(f32[2048,128]{1,0:T(8,128)} %table.1) | copy-start | bytes 3145732
  1.9 0.7 copy-start.1
  2.6 0.7 copy-start.2
  3.3 0.7 copy-start.3

commit v3 on v2

--- a/solution.py
+++ b/solution.py
@@ -22,6 +22,7 @@
 ORDER = (1, 7, 2, 6, 3, 5, 4)
 FAR = (4, 3, 5, 2, 6, 1, 7)
 GROUPS = ((1, 7), (2, 6), (3, 5), (4,))
+SENDS = {(1, 7): (), (2, 6): (), (3, 5): (), (4,): (4, 3, 5, 2, 6, 1, 7)}
 NT = (((1,), (1,)), ((), ()))
 TN = (((0,), (0,)), ((), ()))
 
@@ -69,12 +70,6 @@
 
     sibling = (y * 2 + 1 - core, s)
 
-    barrier = pltpu.get_barrier_semaphore()
-    peers = [zpeer(dz) for dz in range(1, NZ)] + [xpeer(1), xpeer(3), sibling]
-    peers += [ypeer(dy) for dy in range(1, NY)]
-    for peer in peers:
-        pl.semaphore_signal(barrier, inc=1, device_id=peer, device_id_type=MESH)
-
     loads = [
         pltpu.make_async_copy(src, dst, in_sem.at[i])
         for i, (src, dst) in enumerate(
@@ -84,6 +79,12 @@
     for load in loads:
         load.start()
     own.start()
+
+    barrier = pltpu.get_barrier_semaphore()
+    peers = [zpeer(dz) for dz in range(1, NZ)] + [xpeer(1), xpeer(3), sibling]
+    peers += [ypeer(dy) for dy in range(1, NY)]
+    for peer in peers:
+        pl.semaphore_signal(barrier, inc=1, device_id=peer, device_id_type=MESH)
 
     half = TAB // 2
     piece = half // 2
@@ -136,20 +137,18 @@
     row = jnp.where(full, ox, NX + lax.shift_right_logical(ox, 1))
     code_s[...] = jnp.where(used, part * 64 + lax.shift_right_logical(owner, 2) * 8 + row, -1)
     kl_s[...] = pos & 63
-    m1, m2, m3 = split3(conf_ref[...])
-    val_s[0] = (local & 0x700).astype(F32)
-    val_s[1] = (local & 0xFF).astype(F32)
-    val_s[2] = (rowi + 1).astype(F32)
-    val_s[3] = m1.astype(F32)
-    val_s[4] = m2.astype(F32)
-    val_s[5] = m3.astype(F32)
+    m1, m2 = split2(conf_ref[...])
+    val_s[0] = (local & 0xFF).astype(F32)
+    val_s[1] = (rowi * 8 + lax.shift_right_logical(local, 8)).astype(F32)
+    val_s[2] = m1.astype(F32)
+    val_s[3] = m2.astype(F32)
     sub = iota((128, 128), 0)
 
     def build(u, carry):
         cols = pl.ds(pl.multiple_of(u * 128, 128), 128)
         a_s[:, cols] = jnp.where(sub == code_s[pl.ds(u, 1), :], 1.0, 0.0).astype(BF16)
         hot = sub[0:64] == kl_s[pl.ds(u, 1), :]
-        for c in range(6):
+        for c in range(4):
             b_s[c * 64:(c + 1) * 64, cols] = jnp.where(hot, val_s[c, pl.ds(u, 1), :], 0.0).astype(BF16)
         return carry
 
@@ -159,9 +158,10 @@
     def tiles(v):
         return jnp.concatenate([v[:, 0:64], v[:, 64:128]], axis=0).T.reshape(NZ, 8, 128)
 
-    ent_send[:, 0:8, :] = tiles(packed[0:64] + packed[64:128])
-    ent_send[:, 8:16, :] = tiles(packed[128:192])
-    ent_send[:, 16:24, :] = tiles(packed[192:256] + packed[256:320] + packed[320:384])
+    coded = packed[64:128].astype(I32)
+    ent_send[:, 0:8, :] = tiles(packed[0:64] + ((coded & 7) * 256).astype(F32))
+    ent_send[:, 8:16, :] = tiles(lax.shift_right_logical(coded, 3).astype(F32))
+    ent_send[:, 16:24, :] = tiles(packed[128:192] + packed[192:256])
     ent[z] = ent_send[z]
 
     pl.semaphore_wait(barrier, len(peers))
@@ -219,7 +219,7 @@
                 idr[row:row + 1, 512 + t * 128:640 + t * 128] = jnp.where(
                     low, half_row(first, 0, rel, 0), half_row(second, 0, rel, 1))
 
-    ucode = (iota((U, 128), 0) + 1).astype(F32)
+    ucode = iota((U, 128), 0).astype(F32)
     for i in range(NZ):
         for t in range(KH):
             if t < NX:
@@ -231,7 +231,7 @@
                 m = jnp.where(low, half_row(i, 2, first, 0), half_row(i, 2, second, 1))
             eq = user == ucode
             mw[i, :, t * 128:(t + 1) * 128] = jnp.where(eq, m * (1.0 / D), 0.0)
-            mb[i, :, t * 128:(t + 1) * 128] = jnp.where(eq, (1.0 + m) * (1.0 / math.sqrt(D)), 0.0)
+            mb[i, :, t * 128:(t + 1) * 128] = jnp.where(eq & (m > 0.0), (1.0 + m) * (1.0 / math.sqrt(D)), 0.0)
 
     def collect(rel, other):
         def group(g, carry):
@@ -287,12 +287,6 @@
     transpose(tab2, False)
     collect(2, 3)
 
-    scale = 2.0 / ITEMS
-    g = (gacc[0:128, 0:128] + gacc[0:128, 128:256] + gacc[128:256, 0:128] + gacc[128:256, 128:256]) * scale
-    ghl = jnp.concatenate(split2(g), axis=0)
-    for i in range(NZ):
-        ft[i, :, SLOTS:SLOTS + 128] = ghl
-
     def fold(res):
         return res[0:U, 0:128] + res[0:U, 128:256] + res[U:2 * U, 0:128]
 
@@ -338,11 +332,10 @@
         dz: remote(qsend.at[dz, 0:8], qbuf.at[NZ - dz, 0:8], qs_sem.at[dz], qr_sem.at[NZ - dz], zpeer(dz))
         for dz in ORDER}
 
-    def answer(group, fn, copies, rows):
+    def answer(group, fn, rows):
         shares = [fn(lax.rem(z + dz, NZ), dz) for dz in group]
         for dz, value in zip(group, shares):
             qsend[dz, 0:rows] = value
-            copies[dz].start()
 
     def collect_shares(total, copies, rows):
         for dz in ORDER:
@@ -361,14 +354,23 @@
         for group in GROUPS:
             for dz in group:
                 p_copies[NZ - dz].wait_recv()
-            answer(group, lambda i, dz: fn(i, pbuf[i]), copies, rows)
+            answer(group, lambda i, dz: fn(i, pbuf[i]), rows)
+            for dz in SENDS[group]:
+                copies[dz].start()
         total = collect_shares(total, copies, rows)
         for dz in ORDER:
             p_copies[dz].wait_send()
         return total
 
-    answer((4, 3, 5), lambda i, dz: rhs_share(i), q_copies, U)
-    answer((2, 6, 1, 7), lambda i, dz: rhs_share(i), q_copies, U)
+    for group in ((4, 3, 5), (2, 6, 1, 7)):
+        answer(group, lambda i, dz: rhs_share(i), U)
+        for dz in group:
+            q_copies[dz].start()
+    scale = 2.0 / ITEMS
+    g = (gacc[0:128, 0:128] + gacc[0:128, 128:256] + gacc[128:256, 0:128] + gacc[128:256, 128:256]) * scale
+    ghl = jnp.concatenate(split2(g), axis=0)
+    for i in range(NZ):
+        ft[i, :, SLOTS:SLOTS + 128] = ghl
     rhs = collect_shares(rhs_share(z), q_copies, U)
 
     def norm(v):
@@ -427,8 +429,8 @@
         scratch_shapes=[
             pltpu.SMEM((U,), I32), pltpu.VMEM((U, K), I32), pltpu.VMEM((U, K), F32), pltpu.VMEM((1, 512), I32),
             pltpu.VMEM((TAB, D), F32), pltpu.VMEM((TAB, D), F32), pltpu.VMEM((TAB, D), F32), pltpu.VMEM((TAB, D), F32),
-            pltpu.VMEM((U, K), I32), pltpu.VMEM((U, K), I32), pltpu.VMEM((6, U, K), F32),
-            pltpu.VMEM((128, U * K), BF16), pltpu.VMEM((6 * 64, U * K), BF16),
+            pltpu.VMEM((U, K), I32), pltpu.VMEM((U, K), I32), pltpu.VMEM((4, U, K), F32),
+            pltpu.VMEM((128, U * K), BF16), pltpu.VMEM((4 * 64, U * K), BF16),
             pltpu.VMEM((NZ, 24, 128), F32), pltpu.VMEM((NZ, 24, 128), F32), pltpu.VMEM((2, NZ, 24, 128), F32),
             pltpu.VMEM((2 * NX, SLOTS), F32), pltpu.VMEM((2 * D, TAB), BF16), pltpu.VMEM((4, 2 * D, 128), F32),
             pltpu.VMEM((NZ, 2 * D, SLOTS + 128), BF16),
@@ -440,7 +442,7 @@
             dma((NZ,)), dma((NZ,)), dma((NZ,)), dma((NZ,)), dma((NY,)), dma((NY,)), dma((NY,)), dma((NY,)),
         ],
         compiler_params=pltpu.CompilerParams(
-            collective_id=0, has_side_effects=True, vmem_limit_bytes=48 * 1024 * 1024),
+            collective_id=0, has_side_effects=True, vmem_limit_bytes=60 * 1024 * 1024),
     )(valid_counts, neighbours, confidence, row_targets.reshape(1, 512), item_table)
 
 

time: 107 us -> 104 us (0.972)
  local copies, waits for them, and re-layouts: 4.7 us -> 1.67 us
    unnamed x11 -> x1, local copies, waits for them, and re-layouts: 4.7 us -> 1.67 us
where the time goes in v3:
time: 104 us
  Pallas kernels  102 us (98%)
  local copies, waits for them, and re-layouts  1.67 us (2%)
    pallas_call x1, Pallas kernels, per_device(): pl.pallas_call(kernel, out_shape=jax.ShapeDtypeStruct((512, D), F32), in_...  102 us

profile of v3, /device:TPU:1, one launch (start us, length us, event | category | flops | bytes accessed | tf_op | source)
XLA Modules:
  0.0 103.5 jit_solution(208672881974152666)
XLA Ops:
  0.0 101.9 %shard_map.55 = f32[512,128]{1,0:T(8,128)} custom-call(s32[32]{0:T(128)} %counts_hbm.1, s32[32,128]{1,0:T(8,128)} %ids_hbm.1, f32[32,128]{1,0:T(8,128)} %conf_hbm.1, s32[1,512]{1,0:T(1,128)} %bitcast.1, f32[2048,128]{1,0:T(8,128)} %table.1), custom_call_target="tpu_custom_call" | custom-call | tf_op jit(solution)/shard_map/pallas_call | solution.py:424
  101.9 1.7 %copy.7 = f32[512,128]{1,0:T(8,128)} copy(f32[512,128]{1,0:T(8,128)} %shard_map.55) | data formatting | bytes 524288

commit v4 on v3

--- a/solution.py
+++ b/solution.py
@@ -49,7 +49,7 @@
     counts_hbm, ids_hbm, conf_hbm, targ_hbm, table,
     out_ref,
     counts, ids_ref, conf_ref, targ_ref,
-    tab0, tab1, tab2, tab3, code_s, kl_s, val_s, a_s, b_s, ent_send, ent, ent2, idr, tt, halves, ft, mw, mb, gacc,
+    tab0, tab1, tab2, tab3, code_s, kl_s, val_s, a_s, b_s, ent_send, ent, ent2, idr, tt, halves, ft, fn, mw, mb, gacc,
     psend, pbuf, qsend, qbuf, gat, place,
     in_sem, own_sem, tx_sem, trx_sem, tfwd_sem, ts_sem, tsr_sem, es_sem, er_sem, ps_sem, pr_sem, qs_sem, qr_sem,
     ys_sem, yr_sem, ss_sem, sr_sem,
@@ -179,16 +179,17 @@
     loads[3].wait()
     place[...] = jnp.where(iota((512, 512), 0) == targ_ref[...], 1.0, 0.0).astype(BF16)
 
-    def transpose(tab, first):
+    def add_gram(first):
+        g = lax.dot_general(tt[...], tt[...], NT, preferred_element_type=F32)
+        gacc[...] = g if first else gacc[...] + g
+
+    def transpose(tab, first, last=False):
         for c in range(TAB // 128):
             hi, lo = split2(tab[c * 128:(c + 1) * 128, :].T)
             tt[0:128, c * 128:(c + 1) * 128] = hi
             tt[128:256, c * 128:(c + 1) * 128] = lo
-        g = lax.dot_general(tt[...], tt[...], NT, preferred_element_type=F32)
-        if first:
-            gacc[...] = g
-        else:
-            gacc[...] += g
+        if not last:
+            add_gram(first)
 
     own.wait()
     transpose(tab0, True)
@@ -284,7 +285,7 @@
     collect(3, None)
     for i in (4, 5):
         to_sib[i].wait_recv()
-    transpose(tab2, False)
+    transpose(tab2, False, True)
     collect(2, 3)
 
     def fold(res):
@@ -293,12 +294,12 @@
     def rhs_share(i):
         hi, lo = split2(mb[i])
         return fold(lax.dot_general(
-            jnp.concatenate([hi, lo], axis=0), ft[i, :, 0:SLOTS], NT, preferred_element_type=F32))
+            jnp.concatenate([hi, lo], axis=0), ft[i], NT, preferred_element_type=F32))
 
     def project(i, hi, lo):
         lhs = jnp.concatenate(
             [jnp.concatenate([hi, hi], axis=1), jnp.concatenate([lo, jnp.zeros_like(lo)], axis=1)], axis=0)
-        res = jnp.dot(lhs, ft[i, :, 0:SLOTS], preferred_element_type=F32)
+        res = jnp.dot(lhs, ft[i], preferred_element_type=F32)
         return res[0:U] + res[U:2 * U]
 
     def share(i, p):
@@ -306,14 +307,14 @@
         yhi, ylo = split2(mw[i] * project(i, hi, lo))
         lhs = jnp.concatenate(
             [jnp.concatenate([yhi, hi], axis=1), jnp.concatenate([ylo, lo], axis=1)], axis=0)
-        return fold(lax.dot_general(lhs, ft[i], NT, preferred_element_type=F32))
+        return fold(jnp.dot(lhs, fn[i], preferred_element_type=F32))
 
     def last_share(i, p):
         hi, lo = split2(p)
         proj = project(i, hi, lo)
         sq = mw[i] * proj * proj
-        t = fold(lax.dot_general(
-            jnp.concatenate([hi, lo], axis=0), ft[i, :, SLOTS:SLOTS + 128], NT, preferred_element_type=F32)) * p
+        t = fold(jnp.dot(
+            jnp.concatenate([hi, lo], axis=0), fn[i, SLOTS:SLOTS + 128, :], preferred_element_type=F32)) * p
         for kh in range(KH):
             t = t + sq[:, kh * 128:(kh + 1) * 128]
         block = lax.shift_right_logical(iota((8, 128), 1), 5)
@@ -362,15 +363,23 @@
             p_copies[dz].wait_send()
         return total
 
-    for group in ((4, 3, 5), (2, 6, 1, 7)):
+    for group in ((4,), (3, 5), (2, 6), (1, 7)):
         answer(group, lambda i, dz: rhs_share(i), U)
         for dz in group:
             q_copies[dz].start()
+    add_gram(False)
     scale = 2.0 / ITEMS
     g = (gacc[0:128, 0:128] + gacc[0:128, 128:256] + gacc[128:256, 0:128] + gacc[128:256, 128:256]) * scale
-    ghl = jnp.concatenate(split2(g), axis=0)
-    for i in range(NZ):
-        ft[i, :, SLOTS:SLOTS + 128] = ghl
+    gwide = jnp.concatenate(split2(g), axis=1)
+
+    def turn(i, carry):
+        for t in range(KH):
+            cols = slice(t * 128, (t + 1) * 128)
+            fn[i, cols, :] = ft[i, :, cols].astype(F32).T.astype(BF16)
+        fn[i, SLOTS:SLOTS + 128, :] = gwide
+        return carry
+
+    lax.fori_loop(0, NZ, turn, 0)
     rhs = collect_shares(rhs_share(z), q_copies, U)
 
     def norm(v):
@@ -433,7 +442,7 @@
             pltpu.VMEM((128, U * K), BF16), pltpu.VMEM((4 * 64, U * K), BF16),
             pltpu.VMEM((NZ, 24, 128), F32), pltpu.VMEM((NZ, 24, 128), F32), pltpu.VMEM((2, NZ, 24, 128), F32),
             pltpu.VMEM((2 * NX, SLOTS), F32), pltpu.VMEM((2 * D, TAB), BF16), pltpu.VMEM((4, 2 * D, 128), F32),
-            pltpu.VMEM((NZ, 2 * D, SLOTS + 128), BF16),
+            pltpu.VMEM((NZ, 2 * D, SLOTS), BF16), pltpu.VMEM((NZ, SLOTS + 128, 2 * D), BF16),
             pltpu.VMEM((NZ, U, SLOTS), F32), pltpu.VMEM((NZ, U, SLOTS), F32), pltpu.VMEM((2 * D, 2 * D), F32),
             pltpu.VMEM((U, D), F32), pltpu.VMEM((NZ, U, D), F32),
             pltpu.VMEM((NZ, U, D), F32), pltpu.VMEM((NZ, U, D), F32),

time: 104 us -> 102 us (0.981)
  Pallas kernels: 102 us -> 100 us
    pallas_call x1, Pallas kernels: 102 us -> 100 us  [per_device(): pl.pallas_call(kernel, out_shape=jax.ShapeDtypeStruct((512, D), F32), in_...]
where the time goes in v4:
time: 102 us
  Pallas kernels  100 us (98%)
  local copies, waits for them, and re-layouts  1.67 us (2%)
    pallas_call x1, Pallas kernels, per_device(): pl.pallas_call(kernel, out_shape=jax.ShapeDtypeStruct((512, D), F32), in_...  100 us

profile of v4, /device:TPU:1, one launch (start us, length us, event | category | flops | bytes accessed | tf_op | source)
XLA Modules:
  0.0 101.6 jit_solution(6319053943569094917)
XLA Ops:
  0.0 100.0 %shard_map.55 = f32[512,128]{1,0:T(8,128)} custom-call(s32[32]{0:T(128)} %counts_hbm.1, s32[32,128]{1,0:T(8,128)} %ids_hbm.1, f32[32,128]{1,0:T(8,128)} %conf_hbm.1, s32[1,512]{1,0:T(1,128)} %bitcast.1, f32[2048,128]{1,0:T(8,128)} %table.1), custom_call_target="tpu_custom_call" | custom-call | tf_op jit(solution)/shard_map/pallas_call | solution.py:433
  100.0 1.7 %copy.7 = f32[512,128]{1,0:T(8,128)} copy(f32[512,128]{1,0:T(8,128)} %shard_map.55) | data formatting | bytes 524288

commit v5 on v4

--- a/solution.py
+++ b/solution.py
@@ -302,12 +302,20 @@
         res = jnp.dot(lhs, ft[i], preferred_element_type=F32)
         return res[0:U] + res[U:2 * U]
 
-    def share(i, p):
-        hi, lo = split2(p)
-        yhi, ylo = split2(mw[i] * project(i, hi, lo))
-        lhs = jnp.concatenate(
-            [jnp.concatenate([yhi, hi], axis=1), jnp.concatenate([ylo, lo], axis=1)], axis=0)
-        return fold(jnp.dot(lhs, fn[i], preferred_element_type=F32))
+    def share(blocks, vectors):
+        parts = [split2(p) for p in vectors]
+        grams = jnp.dot(
+            jnp.concatenate([v for pair in parts for v in pair], axis=0), fn[0, SLOTS:SLOTS + 128, :],
+            preferred_element_type=F32)
+        out = []
+        for k, (i, (hi, lo)) in enumerate(zip(blocks, parts)):
+            both = jnp.concatenate(split2(mw[i] * project(i, hi, lo)), axis=0)
+            res = jnp.dot(both, fn[i, 0:SLOTS, :], preferred_element_type=F32)
+            out.append(fold(res + grams[2 * U * k:2 * U * (k + 1)]))
+        return out
+
+    def last_shares(blocks, vectors):
+        return [last_share(i, p) for i, p in zip(blocks, vectors)]
 
     def last_share(i, p):
         hi, lo = split2(p)
@@ -334,8 +342,7 @@
         for dz in ORDER}
 
     def answer(group, fn, rows):
-        shares = [fn(lax.rem(z + dz, NZ), dz) for dz in group]
-        for dz, value in zip(group, shares):
+        for dz, value in zip(group, fn([lax.rem(z + dz, NZ) for dz in group])):
             qsend[dz, 0:rows] = value
 
     def collect_shares(total, copies, rows):
@@ -351,11 +358,11 @@
         psend[...] = p
         for dz in FAR:
             p_copies[dz].start()
-        total = fn(z, p)
+        total = fn([z], [p])[0]
         for group in GROUPS:
             for dz in group:
                 p_copies[NZ - dz].wait_recv()
-            answer(group, lambda i, dz: fn(i, pbuf[i]), rows)
+            answer(group, lambda blocks: fn(blocks, [pbuf[i] for i in blocks]), rows)
             for dz in SENDS[group]:
                 copies[dz].start()
         total = collect_shares(total, copies, rows)
@@ -364,7 +371,7 @@
         return total
 
     for group in ((4,), (3, 5), (2, 6), (1, 7)):
-        answer(group, lambda i, dz: rhs_share(i), U)
+        answer(group, lambda blocks: [rhs_share(i) for i in blocks], U)
         for dz in group:
             q_copies[dz].start()
     add_gram(False)
@@ -396,7 +403,7 @@
 
     carry = (jnp.zeros_like(rhs), rhs, rhs, norm(rhs))
     sol, res, p, rr = lax.fori_loop(0, ITERS - 1, iterate, carry)
-    folded = exchange(last_share, p, t_copies, 8)
+    folded = exchange(last_shares, p, t_copies, 8)
     block = lax.shift_right_logical(iota((8, 128), 1), 5)
     pq = norm(p) + jnp.concatenate(
         [jnp.sum(jnp.where(block == c, folded, 0.0), axis=1, keepdims=True) for c in range(4)], axis=0)

time: 102 us -> 103 us (level)
  no operation moved by 1% of the time
where the time goes in v5:
time: 103 us; the launch traced here: 102 us
  Pallas kernels  101 us (98%)
  local copies, waits for them, and re-layouts  1.67 us (2%)
    pallas_call x1, Pallas kernels, per_device(): pl.pallas_call(kernel, out_shape=jax.ShapeDtypeStruct((512, D), F32), in_...  101 us

profile of v5, /device:TPU:1, one launch (start us, length us, event | category | flops | bytes accessed | tf_op | source)
XLA Modules:
  0.0 102.5 jit_solution(539906784615077502)
XLA Ops:
  0.0 100.8 %shard_map.55 = f32[512,128]{1,0:T(8,128)} custom-call(s32[32]{0:T(128)} %counts_hbm.1, s32[32,128]{1,0:T(8,128)} %ids_hbm.1, f32[32,128]{1,0:T(8,128)} %conf_hbm.1, s32[1,512]{1,0:T(1,128)} %bitcast.1, f32[2048,128]{1,0:T(8,128)} %table.1), custom_call_target="tpu_custom_call" | custom-call | tf_op jit(solution)/shard_map/pallas_call | solution.py:440
  100.8 1.7 %copy.7 = f32[512,128]{1,0:T(8,128)} copy(f32[512,128]{1,0:T(8,128)} %shard_map.55) | data formatting | bytes 524288
